TPU v7x, 32 devices: a whole 2x2x4 slice. The times are simulated.
32 devices in a mesh: grp: 4 (over y, core), seq: 8 (over z, x).
Axes of the slice: x: 2, y: 2, z: 4, core: 2. Of those that a mesh axis runs over, the one named last changes fastest.
Arguments:
- queries: bfloat16 [4096, 8192], P(('grp', 'seq')), may hold values from -8 to 8
- image_keys: bfloat16 [2048, 1024], P('grp'), may hold values from -8 to 8
- image_values: bfloat16 [2048, 1024], P('grp'), may hold values from -12 to 12
- gate_logit: float32 [1], replicated, may hold values from 0.5 to 1.5
- block_image: int32 [32, 1], P('grp'), may hold values from 0 to 3
- image_counts: int32 [4], replicated, may hold values from 128 to 512, as said below
- output_grad: bfloat16 [4096, 8192], P(('grp', 'seq')), may hold values from -6 to 6
Outputs:
- attended: bfloat16 [4096, 8192], P(('grp', 'seq'))
- query_grad: bfloat16 [4096, 8192], P(('grp', 'seq'))
- key_grad: bfloat16 [2048, 1024], P(('grp', 'seq'))
- value_grad: bfloat16 [2048, 1024], P(('grp', 'seq'))
Inputs may be any that keep to these rules, and one draw needn't show every extreme that they name: `block_image`: block b covers text rows b * 128 to (b + 1) * 128 - 1; every image is named by some block. `image_counts`: the leading positions of each image's 512 that hold real tokens; some image fills all 512.
All inputs are finite; a program needn't handle non-finite values.
Results may differ from a plain program's by a relative error of at most 0.015.
Values may be sent and summed in bfloat16 or wider, within the bound.
A program may use at most 64 MiB of HBM per device.

v0:
```python
import jax
import jax.numpy as jnp
from jax import lax
from jax.sharding import PartitionSpec as P

H = 64
KVH = 8
DH = 128
SLOT = 512
BLK = 128


def per_device(
    queries, image_keys, image_values, gate_logit, block_image, image_counts, output_grad
):
    text_split = lax.axis_size("seq")
    sharers = text_split // KVH
    heads_here = H // text_split
    scaling = DH ** (-0.5)
    text_index = lax.axis_index("seq")
    shared_head = text_index // sharers
    factor = jnp.tanh(gate_logit[0])
    out_scaled = (factor * output_grad.astype(jnp.float32)).astype(jnp.bfloat16)
    head_query, head_grad = (
        lax.all_to_all(queries, "seq", split_axis=1, concat_axis=0, tiled=True),
        lax.all_to_all(out_scaled, "seq", split_axis=1, concat_axis=0, tiled=True),
    )
    head_columns = jnp.stack(
        [
            lax.dynamic_slice_in_dim(image_keys, shared_head * DH, DH, 1),
            lax.dynamic_slice_in_dim(image_values, shared_head * DH, DH, 1),
        ]
    )
    gathered = lax.all_gather(head_columns, "grp", axis=1, tiled=True)
    rows_here = head_query.shape[0]
    block_count = rows_here // BLK
    positions = jnp.arange(SLOT)
    query_blocks = head_query.reshape(block_count, BLK * heads_here, DH)
    grad_blocks = head_grad.reshape(block_count, BLK * heads_here, DH)
    images = block_image[:, 0]
    contract_rows = (((0,), (0,)), ((), ()))
    contract_cols = (((1,), (1,)), ((), ()))

    def block_step(totals, block_inputs):
        key_total, value_total = totals
        query_rows, grad_rows, image_id = block_inputs
        first_row = image_id * SLOT
        pair_rows = lax.dynamic_slice_in_dim(gathered, first_row, SLOT, 1)
        key_rows = pair_rows[0]
        value_rows = pair_rows[1]
        visible = positions < image_counts[image_id]
        scores = (
            lax.dot_general(query_rows, key_rows, contract_cols, preferred_element_type=jnp.float32)
            * scaling
        )
        scores = jnp.where(visible, scores, -jnp.inf)
        exponent = jnp.exp(scores - jnp.max(scores, axis=1, keepdims=True))
        weights = exponent / jnp.sum(exponent, axis=1, keepdims=True)
        weights_low = weights.astype(jnp.bfloat16)
        mixture = jnp.dot(weights_low, value_rows, preferred_element_type=jnp.float32)
        attended = (factor * mixture).astype(jnp.bfloat16)
        value_term = lax.dot_general(
            weights_low, grad_rows, contract_rows, preferred_element_type=jnp.float32
        )
        weight_grad = lax.dot_general(
            grad_rows, value_rows, contract_cols, preferred_element_type=jnp.float32
        )
        centre = jnp.sum(weights * weight_grad, axis=1, keepdims=True)
        score_grad = (weights * (weight_grad - centre) * scaling).astype(jnp.bfloat16)
        query_term = jnp.dot(score_grad, key_rows, preferred_element_type=jnp.float32).astype(
            jnp.bfloat16
        )
        key_term = lax.dot_general(
            score_grad, query_rows, contract_rows, preferred_element_type=jnp.float32
        )
        key_old = lax.dynamic_slice_in_dim(key_total, first_row, SLOT, 0)
        key_total = lax.dynamic_update_slice_in_dim(key_total, key_old + key_term, first_row, 0)
        value_old = lax.dynamic_slice_in_dim(value_total, first_row, SLOT, 0)
        value_total = lax.dynamic_update_slice_in_dim(
            value_total, value_old + value_term, first_row, 0
        )
        return ((key_total, value_total), (attended, query_term))

    zeros_total = jnp.zeros((gathered.shape[1], DH), jnp.float32)
    totals, outputs = lax.scan(
        block_step, (zeros_total, zeros_total), (query_blocks, grad_blocks, images)
    )
    key_total, value_total = totals
    attended_heads = outputs[0].reshape(rows_here, heads_here * DH)
    query_heads = outputs[1].reshape(rows_here, heads_here * DH)
    attended, query_grad = (
        lax.all_to_all(attended_heads, "seq", split_axis=0, concat_axis=1, tiled=True),
        lax.all_to_all(query_heads, "seq", split_axis=0, concat_axis=1, tiled=True),
    )
    key_part, value_part = (
        lax.psum_scatter(
            key_total.astype(jnp.bfloat16), "grp", scatter_dimension=0, tiled=True
        ).astype(jnp.float32),
        lax.psum_scatter(
            value_total.astype(jnp.bfloat16), "grp", scatter_dimension=0, tiled=True
        ).astype(jnp.float32),
    )
    out_rows = key_part.shape[0] // text_split
    key_pieces, value_pieces = (
        lax.all_to_all(
            key_part.reshape(text_split, out_rows, DH).astype(jnp.bfloat16),
            "seq",
            split_axis=0,
            concat_axis=0,
            tiled=True,
        ).astype(jnp.float32),
        lax.all_to_all(
            value_part.reshape(text_split, out_rows, DH).astype(jnp.bfloat16),
            "seq",
            split_axis=0,
            concat_axis=0,
            tiled=True,
        ).astype(jnp.float32),
    )
    key_heads = key_pieces.reshape(KVH, sharers, out_rows, DH).sum(axis=1)
    value_heads = value_pieces.reshape(KVH, sharers, out_rows, DH).sum(axis=1)
    key_grad = key_heads.transpose(1, 0, 2).reshape(out_rows, KVH * DH).astype(jnp.bfloat16)
    value_grad = value_heads.transpose(1, 0, 2).reshape(out_rows, KVH * DH).astype(jnp.bfloat16)
    return (attended, query_grad, key_grad, value_grad)


def solution(mesh):
    return jax.shard_map(
        per_device,
        mesh=mesh,
        in_specs=(
            P(("grp", "seq"), None),
            P("grp", None),
            P("grp", None),
            P(),
            P("grp", None),
            P(),
            P(("grp", "seq"), None),
        ),
        out_specs=(
            P(("grp", "seq"), None),
            P(("grp", "seq"), None),
            P(("grp", "seq"), None),
            P(("grp", "seq"), None),
        ),
        check_vma=False,
    )
```

profile of v0, /device:TPU:0, one launch (start us, length us, event | category | flops | bytes accessed | tf_op | source)
XLA Modules:
  0.0 425.2 jit_solution(16697520021538045883)
XLA Ops:
  7.2 3.1 copy.36
  10.3 7.3 %all-to-all-start = ((bf16[128,8,1024]{2,0,1:T(8,128)(2,1)}), bf16[128,8,1024]{2,0,1:T(8,128)(2,1)S(1)}, u32[]{:S(2)}, u32[]{:S(2)}) async-start(bf16[128,8,1024]{2,0,1:T(8,128)(2,1)} %bitcast.104), calls=%async_computation | async-start | bytes 4194304 | tf_op jit(solution)/shard_map/all_to_all | solution.py:25
  21.8 44.0 %all-to-all-done = bf16[128,8,1024]{2,0,1:T(8,128)(2,1)S(1)} async-done(((bf16[128,8,1024]{2,0,1:T(8,128)(2,1)}), bf16[128,8,1024]{2,0,1:T(8,128)(2,1)S(1)}, u32[]{:S(2)}, u32[]{:S(2)}) %all-to-all-start) | async-done | bytes 2097184 | tf_op jit(solution)/shard_map/all_to_all | solution.py:25
  67.1 4.3 %all-to-all-start.1 = ((bf16[128,8,1024]{2,0,1:T(8,128)(2,1)}), bf16[128,8,1024]{2,0,1:T(8,128)(2,1)}, u32[]{:S(2)}, u32[]{:S(2)}) async-start(bf16[128,8,1024]{2,0,1:T(8,128)(2,1)} %bitcast.103), calls=%async_computation.1 | async-start | bytes 4194304 | tf_op jit(solution)/shard_map/all_to_all | solution.py:26
  73.4 2.8 reshape.50
  76.2 43.1 %all-to-all-done.1 = bf16[128,8,1024]{2,0,1:T(8,128)(2,1)} async-done(((bf16[128,8,1024]{2,0,1:T(8,128)(2,1)}), bf16[128,8,1024]{2,0,1:T(8,128)(2,1)}, u32[]{:S(2)}, u32[]{:S(2)}) %all-to-all-start.1) | async-done | bytes 2097184 | tf_op jit(solution)/shard_map/all_to_all | solution.py:26
  119.3 4.2 reshape.51
  124.6 126.4 %while.17 = (s32[]{:T(128)}, f32[2048,128]{1,0:T(8,128)S(1)}, f32[2048,128]{1,0:T(8,128)}, bf16[8,1024,128]{2,1,0:T(8,128)(2,1)}, bf16[8,1024,128]{2,1,0:T(8,128...) while((s32[]{:T(128)}, f32[2048,128]{1,0:T(8,128)S(1)}, ...), condition=%wide.region_4.5_spmd.clone, body=%wide.region_0.4_spmd.clone.sunk | while | flops 822081024 | bytes 23126356 | solution.py:85
  133.0 2.5 fusion.58
  148.7 2.5 fusion.58
  164.5 2.5 fusion.58
  253.3 19.4 %reduce-scatter.3.cloned.1.call-done = bf16[512,128]{1,0:T(8,128)(2,1)} async-done(((bf16[2048,128]{1,0:T(8,128)(2,1)}), bf16[512,128]{1,0:T(8,128)(2,1)}) %reduce-scatter.3.cloned.1.call-update) | async-done | bytes 131088 | tf_op jit(solution)/shard_map/reduce_scatter | solution.py:96
  272.7 5.5 %all-to-all-start.4 = ((bf16[8,64,128]{2,1,0:T(8,128)(2,1)}), bf16[8,64,128]{2,1,0:T(8,128)(2,1)S(1)}, u32[]{:S(2)}, u32[]{:S(2)}) async-start(bf16[8,64,128]{2,1,0:T(8,128)(2,1)} %bitcast.109), calls=%async_computation.5 | async-start | bytes 262144 | tf_op jit(solution)/shard_map/all_to_all | solution.py:105
  278.2 18.8 %reduce-scatter.5.cloned.1.call-done = bf16[512,128]{1,0:T(8,128)(2,1)} async-done(((bf16[2048,128]{1,0:T(8,128)(2,1)}), bf16[512,128]{1,0:T(8,128)(2,1)}) %reduce-scatter.5.cloned.1.call-update) | async-done | bytes 131088 | tf_op jit(solution)/shard_map/reduce_scatter | solution.py:99
  297.1 5.5 %all-to-all-start.5 = ((bf16[8,64,128]{2,1,0:T(8,128)(2,1)}), bf16[8,64,128]{2,1,0:T(8,128)(2,1)S(1)}, u32[]{:S(2)}, u32[]{:S(2)}) async-start(bf16[8,64,128]{2,1,0:T(8,128)(2,1)} %bitcast.110), calls=%async_computation.7 | async-start | bytes 262144 | tf_op jit(solution)/shard_map/all_to_all | solution.py:112
  304.9 5.0 %all-to-all-done.5 = bf16[8,64,128]{2,1,0:T(8,128)(2,1)S(1)} async-done(((bf16[8,64,128]{2,1,0:T(8,128)(2,1)}), bf16[8,64,128]{2,1,0:T(8,128)(2,1)S(1)}, u32[]{:S(2)}, u32[]{:S(2)}) %all-to-all-start.5) | async-done | bytes 131104 | tf_op jit(solution)/shard_map/all_to_all | solution.py:112
  309.9 3.6 all-to-all-start.3
  313.5 4.2 all_to_all.64
  317.7 42.9 %all-to-all-done.3 = bf16[8,128,1024]{2,1,0:T(8,128)(2,1)S(1)} async-done(((bf16[8,128,1024]{2,1,0:T(8,128)(2,1)}), bf16[8,128,1024]{2,1,0:T(8,128)(2,1)S(1)}, u32[]{:S(2)}, u32[]{:S(2)}) %all-to-all-start.3) | async-done | bytes 2097184 | tf_op jit(solution)/shard_map/all_to_all | solution.py:93
  360.6 4.3 %all-to-all-start.2 = ((bf16[8,128,1024]{2,1,0:T(8,128)(2,1)}), bf16[8,128,1024]{2,1,0:T(8,128)(2,1)}, u32[]{:S(2)}, u32[]{:S(2)}) async-start(bf16[8,128,1024]{2,1,0:T(8,128)(2,1)} %all_to_all.64), calls=%async_computation.2 | async-start | bytes 4194304 | tf_op jit(solution)/shard_map/all_to_all | solution.py:92
  368.6 4.1 copy.26
  372.7 40.0 %all-to-all-done.2 = bf16[8,128,1024]{2,1,0:T(8,128)(2,1)} async-done(((bf16[8,128,1024]{2,1,0:T(8,128)(2,1)}), bf16[8,128,1024]{2,1,0:T(8,128)(2,1)}, u32[]{:S(2)}, u32[]{:S(2)}) %all-to-all-start.2) | async-done | bytes 2097184 | tf_op jit(solution)/shard_map/all_to_all | solution.py:92
  412.7 3.0 copy.21
  415.8 2.9 copy.25
  (117 shorter events, 116.8 us)
Async XLA Ops:
  10.3 55.5 %all-to-all-start = ((bf16[128,8,1024]{2,0,1:T(8,128)(2,1)}), bf16[128,8,1024]{2,0,1:T(8,128)(2,1)S(1)}, u32[]{:S(2)}, u32[]{:S(2)}) async-start(bf16[128,8,1024]{2,0,1:T(8,128)(2,1)} %bitcast.104), calls=%async_computation | async-start | bytes 4194304 | tf_op jit(solution)/shard_map/all_to_all | solution.py:25
  65.8 1.3 copy-start
  67.1 52.2 %all-to-all-start.1 = ((bf16[128,8,1024]{2,0,1:T(8,128)(2,1)}), bf16[128,8,1024]{2,0,1:T(8,128)(2,1)}, u32[]{:S(2)}, u32[]{:S(2)}) async-start(bf16[128,8,1024]{2,0,1:T(8,128)(2,1)} %bitcast.103), calls=%async_computation.1 | async-start | bytes 4194304 | tf_op jit(solution)/shard_map/all_to_all | solution.py:26
  71.5 52.0 %all-gather.2.cloned.1.call-start = ((), (), s32[]{:S(2)}) async-start(), calls=%async_computation.8 | async-start | bytes 1310720 | tf_op jit(solution)/shard_map/all_gather | solution.py:34
  73.3 199.4 %reduce-scatter.3.cloned.1.call-start = ((), (), s32[]{:S(2)}) async-start(), calls=%async_computation.9 | async-start | bytes 655360 | tf_op jit(solution)/shard_map/reduce_scatter | solution.py:96
  123.5 1.1 copy-start.3
  123.5 1.1 copy-start.4
  251.0 1.4 copy-start.1
  251.8 50.8 %copy-start.2 = (bf16[8,1024,128]{2,1,0:T(8,128)(2,1)S(1)}, bf16[8,1024,128]{2,1,0:T(8,128)(2,1)}, u32[]{:S(2)}) copy-start(bf16[8,1024,128]{2,1,0:T(8,128)(2,1)} %get-tuple-element.70) | copy-start | bytes 6291460
  251.9 45.2 %reduce-scatter.5.cloned.1.call-start = ((), (), s32[]{:S(2)}) async-start(), calls=%async_computation.10 | async-start | bytes 655360 | tf_op jit(solution)/shard_map/reduce_scatter | solution.py:99
  272.7 24.4 %all-to-all-start.4 = ((bf16[8,64,128]{2,1,0:T(8,128)(2,1)}), bf16[8,64,128]{2,1,0:T(8,128)(2,1)S(1)}, u32[]{:S(2)}, u32[]{:S(2)}) async-start(bf16[8,64,128]{2,1,0:T(8,128)(2,1)} %bitcast.109), calls=%async_computation.5 | async-start | bytes 262144 | tf_op jit(solution)/shard_map/all_to_all | solution.py:105
  297.1 12.9 %all-to-all-start.5 = ((bf16[8,64,128]{2,1,0:T(8,128)(2,1)}), bf16[8,64,128]{2,1,0:T(8,128)(2,1)S(1)}, u32[]{:S(2)}, u32[]{:S(2)}) async-start(bf16[8,64,128]{2,1,0:T(8,128)(2,1)} %bitcast.110), calls=%async_computation.7 | async-start | bytes 262144 | tf_op jit(solution)/shard_map/all_to_all | solution.py:112
  309.9 50.6 %all-to-all-start.3 = ((bf16[8,128,1024]{2,1,0:T(8,128)(2,1)}), bf16[8,128,1024]{2,1,0:T(8,128)(2,1)S(1)}, u32[]{:S(2)}, u32[]{:S(2)}) async-start(bf16[8,128,1024]{2,1,0:T(8,128)(2,1)} %all_to_all.68), calls=%async_computation.3 | async-start | bytes 4194304 | tf_op jit(solution)/shard_map/all_to_all | solution.py:93
  360.6 52.2 %all-to-all-start.2 = ((bf16[8,128,1024]{2,1,0:T(8,128)(2,1)}), bf16[8,128,1024]{2,1,0:T(8,128)(2,1)}, u32[]{:S(2)}, u32[]{:S(2)}) async-start(bf16[8,128,1024]{2,1,0:T(8,128)(2,1)} %all_to_all.64), calls=%async_computation.2 | async-start | bytes 4194304 | tf_op jit(solution)/shard_map/all_to_all | solution.py:92
Sparse Core Ops, SparseCore 0:
  73.9 18.0 all-gather.1
  252.0 20.6 reduce-scatter.2
  275.4 21.6 reduce-scatter.4
where the time goes:
time: 427 us; the launch traced here: 425 us
  waiting for transfers between devices  213 us (50%)
  matrix products  84.5 us (20%)
  local copies, waits for them, and re-layouts  45.1 us (11%)
  starting transfers between devices  30.7 us (7%)
  other arithmetic  18.6 us (4%)
  loops' own time  18.3 us (4%)
  between operations  14.5 us (3%)
    all_to_all x1, waiting for transfers between devices, per_device(): lax.all_to_all(queries, 'seq', split_axis=1, concat_axis=0, tiled=True)  44 us
    all_to_all x1, waiting for transfers between devices, per_device(): lax.all_to_all(out_scaled, 'seq', split_axis=1, concat_axis=0, tiled=True)  43.1 us
    all_to_all x1, waiting for transfers between devices, per_device(): lax.all_to_all(query_heads, 'seq', split_axis=0, concat_axis=1, tiled=True)  42.9 us
    all_to_all x1, waiting for transfers between devices, per_device(): lax.all_to_all(attended_heads, 'seq', split_axis=0, concat_axis=1, tiled=...  40 us
    dot_general x8, matrix products, block_step(): jnp.dot(weights_low, value_rows, preferred_element_type=jnp.float32)  19.7 us
    dot_general x8, matrix products, block_step(): lax.dot_general(weights_low, grad_rows, contract_rows, preferred_element_...  19.6 us
    reduce_scatter x1, waiting for transfers between devices, per_device(): lax.psum_scatter(key_total.astype(jnp.bfloat16), 'grp', scatter_dimension...  19.4 us
    reduce_scatter x1, waiting for transfers between devices, per_device(): lax.psum_scatter(value_total.astype(jnp.bfloat16), 'grp', scatter_dimensi...  18.8 us
  transfers between devices with their start and end apart: 9, of which 7 were waited for; matrix products, arithmetic and copies ran while one was open for 5% of the time, Pallas kernels for 0%

commit v1 on v0

v1 whole, which is shorter than its diff:
```python
import functools
import math

import jax
import jax.numpy as jnp
from jax import lax
from jax.experimental import pallas as pl
from jax.experimental.pallas import tpu as pltpu
from jax.sharding import PartitionSpec as P

KVH = 8
DH = 128
SLOT = 512
IMAGES = 4
BLK = 128
GROUPS = 8
PAIR = 2
SCALE = DH**-0.5
LOG2E = math.log2(math.e)

ROWS = (((1,), (1,)), ((), ()))


def dot(a, b, dims=(((1,), (0,)), ((), ()))):
    return lax.dot_general(a, b, dims, preferred_element_type=jnp.float32)


def attend(ids, counts, gate_ref, q_ref, g_ref, k_ref, v_ref, o_ref, dq_ref, dkv_ref):
    count = counts[ids[pl.program_id(0)]]
    factor = jnp.tanh(jnp.full((1, DH), gate_ref[0], jnp.float32))
    keys, values = k_ref[...], v_ref[...]
    keys_t, values_t = keys.T, values.T
    wide = PAIR * BLK
    visible = lax.broadcasted_iota(jnp.int32, (SLOT, wide), 0) < count
    dk = jnp.zeros((SLOT, DH), jnp.float32)
    dv = jnp.zeros((SLOT, DH), jnp.float32)
    for first in range(0, GROUPS, PAIR):
        heads = [slice(h * DH, (h + 1) * DH) for h in range(first, first + PAIR)]
        q = jnp.concatenate([q_ref[:, h] for h in heads], axis=0)
        g = jnp.concatenate(
            [(g_ref[:, h].astype(jnp.float32) * factor).astype(jnp.bfloat16) for h in heads], axis=0
        )
        scores = jnp.where(visible, dot(keys, q, ROWS), -jnp.inf)
        top = jnp.max(scores, axis=0, keepdims=True)
        expo = jnp.exp2((scores - top) * (SCALE * LOG2E))
        weights = expo * (1.0 / jnp.sum(expo, axis=0, keepdims=True))
        low = weights.astype(jnp.bfloat16)
        dv += dot(low, g)
        o_t = dot(values_t, low)
        wgrad = dot(values, g, ROWS)
        centre = jnp.sum(weights * wgrad, axis=0, keepdims=True)
        sgrad = (weights * (wgrad - centre)).astype(jnp.bfloat16)
        dq_t = dot(keys_t, sgrad)
        dk += dot(sgrad, q)
        for i, h in enumerate(heads):
            cols = slice(i * BLK, (i + 1) * BLK)
            o_ref[:, h] = (o_t[:, cols].T * factor).astype(jnp.bfloat16)
            dq_ref[:, h] = (dq_t[:, cols].T * SCALE).astype(jnp.bfloat16)
    dkv_ref[0, :, :DH] = (dk * SCALE).astype(jnp.bfloat16)
    dkv_ref[0, :, DH:] = dv.astype(jnp.bfloat16)


def attention(ids, counts, gate, q, g, k, v):
    rows = q.shape[0]
    blocks = rows // BLK
    row_spec = pl.BlockSpec((BLK, GROUPS * DH), lambda b, j, ids, counts: (b, j))
    image_spec = pl.BlockSpec((SLOT, DH), lambda b, j, ids, counts: (ids[b], j))
    return pl.pallas_call(
        attend,
        grid_spec=pltpu.PrefetchScalarGridSpec(
            num_scalar_prefetch=2,
            grid=(blocks, KVH),
            in_specs=[
                pl.BlockSpec(memory_space=pltpu.SMEM),
                row_spec,
                row_spec,
                image_spec,
                image_spec,
            ],
            out_specs=[
                row_spec,
                row_spec,
                pl.BlockSpec((1, SLOT, 2 * DH), lambda b, j, ids, counts: (b, 0, j)),
            ],
        ),
        out_shape=[
            jax.ShapeDtypeStruct(q.shape, jnp.bfloat16),
            jax.ShapeDtypeStruct(q.shape, jnp.bfloat16),
            jax.ShapeDtypeStruct((blocks, SLOT, 2 * KVH * DH), jnp.bfloat16),
        ],
        compiler_params=pltpu.CompilerParams(vmem_limit_bytes=40 << 20),
        cost_estimate=pl.CostEstimate(
            flops=12 * rows * KVH * GROUPS * SLOT * DH,
            bytes_accessed=16 << 20,
            transcendentals=rows * KVH * GROUPS * SLOT,
        ),
    )(ids, counts, gate, q, g, k, v)


def per_device(queries, image_keys, image_values, gate_logit, block_image, image_counts, output_grad):
    grp, seq = lax.axis_size("grp"), lax.axis_size("seq")
    keys = lax.all_gather(image_keys, "grp", axis=0, tiled=True)
    values = lax.all_gather(image_values, "grp", axis=0, tiled=True)
    blocks = queries.shape[0] // BLK
    ids_all = lax.all_gather(block_image[:, 0], "grp", axis=0, tiled=True).reshape(grp, seq, blocks)
    ids_here = lax.dynamic_index_in_dim(ids_all, lax.axis_index("seq"), 1, keepdims=False)
    ids = lax.dynamic_slice_in_dim(block_image[:, 0], lax.axis_index("seq") * blocks, blocks, 0)
    attended, query_grad, dkv = attention(
        ids, image_counts, gate_logit, queries, output_grad, keys, values
    )
    cols = dkv.shape[2] // grp
    parts = lax.all_to_all(
        dkv.reshape(blocks, SLOT, grp, cols), "grp", split_axis=2, concat_axis=0, tiled=True
    )
    parts = parts.reshape(grp * blocks, SLOT, cols)
    flat_ids = ids_here.reshape(grp * blocks)
    picked = [
        jnp.where((flat_ids == m)[:, None, None], parts.astype(jnp.float32), 0.0).sum(0)
        for m in range(IMAGES)
    ]
    out_rows = IMAGES * SLOT // (grp * seq)
    dense = jnp.stack(picked).astype(jnp.bfloat16).reshape(grp, seq, out_rows, cols)
    mine = lax.psum_scatter(dense, "seq", scatter_dimension=1, tiled=True)
    mine = mine.reshape(grp, out_rows, cols)
    whole = lax.all_to_all(mine, "grp", split_axis=0, concat_axis=0, tiled=True)
    whole = whole.transpose(1, 0, 2).reshape(out_rows, KVH, 2, DH)
    key_grad = whole[:, :, 0].reshape(out_rows, KVH * DH)
    value_grad = whole[:, :, 1].reshape(out_rows, KVH * DH)
    return attended, query_grad, key_grad, value_grad


def solution(mesh):
    rows = P(("grp", "seq"), None)
    return jax.shard_map(
        per_device,
        mesh=mesh,
        in_specs=(rows, P("grp", None), P("grp", None), P(), P("grp", None), P(), rows),
        out_specs=(rows, rows, rows, rows),
        check_vma=False,
    )
```

time: 427 us -> 275 us (0.64)
  matrix products: 84.5 us -> 0 us
  waiting for transfers between devices: 213 us -> 175 us
  local copies, waits for them, and re-layouts: 45.1 us -> 11.9 us
  blocking collectives: 0 us -> 32.8 us
  Pallas kernels: 0 us -> 32.3 us
  starting transfers between devices: 30.7 us -> 3.86 us
  loops' own time: 18.3 us -> 0 us
  other arithmetic: 18.6 us -> 3.35 us
    all_to_all x6 -> x1, waiting for transfers between devices: 175 us -> 0.01 us  [per_device(): lax.all_to_all(dkv.reshape(blocks, SLOT, grp, cols), 'grp', split_axis=2,...]
    unnamed x3 -> x4, waiting for transfers between devices: 0.05 us -> 102 us
    dot_general x48 -> x0, matrix products: 84.5 us -> none  [the longest x8 19.7 us: block_step(): jnp.dot(weights_low, value_rows, preferred_element_type=jnp.float32)]
    all_gather x1 -> x2, waiting for transfers between devices: 0.01 us -> 73 us  [the longest x1 36.9 us: per_device(): keys = lax.all_gather(image_keys, 'grp', axis=0, tiled=True)]
    reduce_scatter x2 -> x0, waiting for transfers between devices: 38.3 us -> none  [the longest x1 19.4 us: per_device(): lax.psum_scatter(key_total.astype(jnp.bfloat16), 'grp', scatter_dimension...]
    pallas_call x0 -> x1, Pallas kernels: none -> 32.3 us  [attention(): pl.pallas_call(attend, grid_spec=pltpu.PrefetchScalarGridSpec(num_scalar_...]
    all_to_all x6 -> x1, starting transfers between devices: 30.6 us -> 3.74 us  [per_device(): lax.all_to_all(dkv.reshape(blocks, SLOT, grp, cols), 'grp', split_axis=2,...]
    unnamed x0 -> x1, blocking collectives: none -> 24.3 us
  transfers between devices with their start and end apart: 9 -> 4, of which waited for: 7 -> 3; matrix products, arithmetic and copies ran while one was open for 5% -> 1% of each run, Pallas kernels for 0% -> 0%
where the time goes in v1:
time: 275 us
  waiting for transfers between devices  175 us (64%)
  blocking collectives  32.8 us (12%)
  Pallas kernels  32.3 us (12%)
  between operations  15.2 us (6%)
  local copies, waits for them, and re-layouts  11.9 us (4%)
  starting transfers between devices  3.86 us (1%)
  other arithmetic  3.35 us (1%)
    unnamed x4, waiting for transfers between devices  102 us
    all_gather x1, waiting for transfers between devices, per_device(): keys = lax.all_gather(image_keys, 'grp', axis=0, tiled=True)  36.9 us
    all_gather x1, waiting for transfers between devices, per_device(): values = lax.all_gather(image_values, 'grp', axis=0, tiled=True)  36.1 us
    pallas_call x1, Pallas kernels, attention(): pl.pallas_call(attend, grid_spec=pltpu.PrefetchScalarGridSpec(num_scalar_...  32.3 us
    unnamed x1, blocking collectives  24.3 us
    all_to_all x1, blocking collectives, per_device(): whole = lax.all_to_all(mine, 'grp', split_axis=0, concat_axis=0, tiled=True)  8.58 us
    unnamed x18, local copies, waits for them, and re-layouts  5.69 us
  transfers between devices with their start and end apart: 4, of which 3 were waited for; matrix products, arithmetic and copies ran while one was open for 1% of the time, Pallas kernels for 0%

profile of v1, /device:TPU:0, one launch (start us, length us, event | category | flops | bytes accessed | tf_op | source)
XLA Modules:
  0.0 274.5 jit_solution(12338507576824525700)
XLA Ops:
  7.2 0.7 all-gather.4.cloned.1.call-update
  8.0 0.7 all-gather.6.cloned.1.call-update
  9.3 0.6 constant_dynamic-slice_fusion
  9.9 36.9 %all-gather.4.cloned.1.call-done.k_ref = bf16[2048,1024]{1,0:T(8,128)(2,1)} async-done(((bf16[512,1024]{1,0:T(8,128)(2,1)}), bf16[2048,1024]{1,0:T(8,128)(2,1)}) %all-gather.4.cloned.1.call-update) | async-done | bytes 4194320 | tf_op jit(solution)/shard_map/all_gather | solution.py:102
  46.8 36.1 %all-gather.6.cloned.1.call-done.v_ref = bf16[2048,1024]{1,0:T(8,128)(2,1)} async-done(((bf16[512,1024]{1,0:T(8,128)(2,1)}), bf16[2048,1024]{1,0:T(8,128)(2,1)}) %all-gather.6.cloned.1.call-update) | async-done | bytes 4194320 | tf_op jit(solution)/shard_map/all_gather | solution.py:103
  82.9 2.2 copy-done
  85.1 1.6 copy-done.2
  86.7 32.3 %shard_map.102 = (bf16[128,8192]{1,0:T(8,128)(2,1)}, bf16[128,8192]{1,0:T(8,128)(2,1)}, bf16[1,512,2048]{2,1,0:T(8,128)(2,1)S(1)}) custom-call(s32[1]{0:T(128)} %bitcast.6.ids, s32[4]{0:T(128)S(1)} %copy-done.3, f32[1]{0:T(128)S(6)} %copy.25.gate_ref, bf16[128,8192]{1,0:T(8,128)(2,1)S(1)} %copy-done.1, bf16[128,8192]{1,0:T(8,128)(2,1)S(1)} %copy-done.2, ...), custom_call_target="tpu_custom_call" | custom-call | flops 6442450944 | bytes 16777216 | tf_op jit(solution)/shard_map/pallas_call | solution.py:68
  118.9 1.5 copy.22
  120.5 3.7 %all-to-all-start = ((bf16[1,512,4,512]{3,1,0,2:T(8,128)(2,1)}), bf16[1,512,4,512]{3,1,0,2:T(8,128)(2,1)S(1)}, u32[]{:S(2)}, u32[]{:S(2)}) async-start(bf16[1,512,4,512]{3,1,0,2:T(8,128)(2,1)} %bitcast.50), calls=%async_computation | async-start | bytes 4194304 | tf_op jit(solution)/shard_map/all_to_all | solution.py:112
  124.3 0.6 dynamic-slice.1
  125.7 24.3 %all-reduce.1 = s32[4,8,1]{1,0,2:T(4,128)S(1)} all-reduce(s32[4,8,1]{1,0,2:T(4,128)S(1)} %reshape.42), channel_id=2, replica_groups=mesh['grp'=4,'seq'=8] {'grp'}, use_global_device_ids=true, to_apply=%add | all-reduce | flops 32 | bytes 256
  150.0 0.2 compare_reduce_fusion.3
  150.2 1.6 fusion
  151.8 1.6 pad_maximum_fusion
  153.4 0.6 copy-done.5
  154.0 0.6 dynamic-slice.2
  154.6 100.7 %all-reduce.5.cloned.1.call-done = bf16[4,8,64,512]{3,2,1,0:T(8,128)(2,1)} async-done(((bf16[4,8,64,512]{3,2,1,0:T(8,128)(2,1)}), bf16[4,8,64,512]{3,2,1,0:T(8,128)(2,1)}) %all-reduce.5.cloned.1.call-update) | async-done | bytes 2097168
  255.3 1.6 dynamic-slice_bitcast_fusion
  257.0 8.6 %all_to_all.14 = bf16[4,64,512]{2,1,0:T(8,128)(2,1)S(1)} all-to-all(bf16[4,64,512]{2,1,0:T(8,128)(2,1)S(1)} %dynamic-slice_bitcast_fusion), channel_id=1, replica_groups=mesh['grp'=4,'seq'=8] {'grp'}, dimensions={0} | all-to-all | bytes 524288 | tf_op jit(solution)/shard_map/all_to_all | solution.py:125
  265.5 0.2 copy.13
  265.7 0.1 reshape.45
  265.9 1.4 slice_reduce_fusion
  267.2 0.7 copy_bitcast_fusion.1
  (19 shorter events, 0.3 us)
Async XLA Ops:
  7.2 2.2 copy-start.4
  7.2 75.7 %copy-start.3 = (s32[4]{0:T(128)S(1)}, s32[4]{0:T(128)}, u32[]{:S(2)}) copy-start(s32[4]{0:T(128)} %counts.1) | copy-start | bytes 52
  7.2 75.7 %copy-start.1 = (bf16[128,8192]{1,0:T(8,128)(2,1)S(1)}, bf16[128,8192]{1,0:T(8,128)(2,1)}, u32[]{:S(2)}) copy-start(bf16[128,8192]{1,0:T(8,128)(2,1)} %q_ref.1) | copy-start | bytes 6291460
  7.2 39.6 %all-gather.4.cloned.1.call-start = ((), (), s32[]{:S(2)}) async-start(), calls=%async_computation.2 | async-start | bytes 5242880 | tf_op jit(solution)/shard_map/all_gather | solution.py:102
  7.9 75.0 %all-gather.6.cloned.1.call-start = ((), (), s32[]{:S(2)}) async-start(), calls=%async_computation.3 | async-start | bytes 5242880 | tf_op jit(solution)/shard_map/all_gather | solution.py:103
  82.9 2.2 copy-start
  85.1 1.6 copy-start.2
  120.5 3.8 %copy-start.6 = (u32[32]{0:T(128)S(1)}, u32[32]{0:T(128)}, u32[]{:S(2)}) copy-start(u32[32]{0:T(128)} %constant.24) | copy-start | bytes 388
  120.5 29.7 %all-to-all-start = ((bf16[1,512,4,512]{3,1,0,2:T(8,128)(2,1)}), bf16[1,512,4,512]{3,1,0,2:T(8,128)(2,1)S(1)}, u32[]{:S(2)}, u32[]{:S(2)}) async-start(bf16[1,512,4,512]{3,1,0,2:T(8,128)(2,1)} %bitcast.50), calls=%async_computation | async-start | bytes 4194304 | tf_op jit(solution)/shard_map/all_to_all | solution.py:112
  124.2 131.1 %all-reduce.5.cloned.1.call-start = ((), (), s32[]{:S(2)}) async-start(), calls=%async_computation.4 | async-start | bytes 4194304
  153.4 0.7 copy-start.5
Sparse Core Ops, SparseCore 0:
  9.6 37.1 all-gather.3
  48.4 34.4 all-gather.5
  153.5 101.7 all-reduce.4

commit v2 on v1

v2 whole, which is shorter than its diff:
```python
import functools
import math

import jax
import jax.numpy as jnp
from jax import lax
from jax.experimental import pallas as pl
from jax.experimental.pallas import tpu as pltpu
from jax.sharding import PartitionSpec as P

KVH = 8
DH = 128
SLOT = 512
IMAGES = 4
BLK = 128
GROUPS = 8
PAIR = 2
SCALE = DH**-0.5
LOG2E = math.log2(math.e)
MESH = pl.DeviceIdType.MESH

ROWS = (((1,), (1,)), ((), ()))


def dot(a, b, dims=(((1,), (0,)), ((), ()))):
    return lax.dot_general(a, b, dims, preferred_element_type=jnp.float32)


def remote(src, dst, send, recv, device):
    return pltpu.make_async_remote_copy(
        src_ref=src, dst_ref=dst, send_sem=send, recv_sem=recv, device_id=device, device_id_type=MESH
    )


def kernel(
    G, S,
    ids_ref, counts_ref, gate_ref, q_ref, g_ref, k_ref, v_ref,
    o_ref, dq_ref, grads_ref,
    kv, idbuf, parts, landed, zsend, zrecv, fsend,
    id_send, id_recv, sib_send, sib_recv, y_send, y_recv, ys_send, ys_recv,
    x_send, x_recv, xs_send, xs_recv, p_send, p_recv, z_send, z_recv, f_send, f_recv,
):
    C, Z = G // 2, S // 2
    GPI = G // IMAGES
    g, s = lax.axis_index("grp"), lax.axis_index("seq")
    c, k = g // 2, g % 2
    zz, x = s // 2, s % 2
    sib = (c * 2 + (1 - k), s)
    xnb = (g, zz * 2 + (1 - x))
    peers = [((g + d // 2) % G, zz * 2 + (x + d) % 2) for d in range(1, 2 * G)]
    zpeers = [(g, ((zz + d) % Z) * 2 + x) for d in range(1, Z)]

    half = k_ref.shape[0] // 2
    for j in range(KVH):
        for h in range(2):
            kv[j, g, h, 0] = k_ref[h * half : (h + 1) * half, j * DH : (j + 1) * DH]
            kv[j, g, h, 1] = v_ref[h * half : (h + 1) * half, j * DH : (j + 1) * DH]
    own = ids_ref[s, 0]
    me = g * 2 + x
    idbuf[me] = jnp.full((8, DH), own, jnp.int32)

    barrier = pltpu.get_barrier_semaphore()
    for device in peers + zpeers:
        pl.semaphore_signal(barrier, inc=1, device_id=device, device_id_type=MESH)
    pl.semaphore_wait(barrier, len(peers) + len(zpeers))

    def sib_copy(j):
        return remote(kv.at[j, g], kv.at[j, g], sib_send.at[j], sib_recv.at[j], sib)

    def y_copy(j, d):
        to = (((c + d) % C) * 2 + k, s)
        return remote(kv.at[j, g, x], kv.at[j, g, x], y_send.at[j, d - 1], y_recv.at[j, d - 1], to)

    def source(d):
        return ((c + C - d) % C) * 2 + k

    def ys_copy(j, d):
        ref = kv.at[j, source(d), x]
        return remote(ref, ref, ys_send.at[j, d - 1], ys_recv.at[j, d - 1], sib)

    def x_copy(j, d):
        ref = kv.at[j, source(d), x]
        return remote(ref, ref, x_send.at[j, d - 1], x_recv.at[j, d - 1], xnb)

    def xs_copy(j, d):
        ref = kv.at[j, source(d), 1 - x]
        return remote(ref, ref, xs_send.at[j, d - 1], xs_recv.at[j, d - 1], sib)

    def id_copy(i):
        return remote(idbuf.at[me], idbuf.at[me], id_send.at[i], id_recv.at[i], peers[i])

    @pl.loop(0, KVH)
    def _(j):
        for d in range(1, C):
            y_copy(j, d).start()
        sib_copy(j).start()

    for i in range(len(peers)):
        id_copy(i).start()

    def y_forward(j):
        for d in range(1, C):
            y_copy(j, d).wait_recv()
            x_copy(j, d).start()
            ys_copy(j, d).start()

    def x_forward(j):
        for d in range(1, C):
            x_copy(j, d).wait_recv()
            xs_copy(j, d).start()

    y_forward(0)
    y_forward(1)
    x_forward(0)
    for i in range(len(peers)):
        id_copy(i).wait()

    count = counts_ref[0]
    for m in range(1, IMAGES):
        count = jnp.where(own == m, counts_ref[m], count)
    factor = jnp.tanh(jnp.full((1, DH), gate_ref[0], jnp.float32))

    def image_of(j, t):
        rows = []
        for i in range(GPI):
            for h in range(2):
                part = kv[j, i, h, t]
                for m in range(1, IMAGES):
                    part = jnp.where(own == m, kv[j, m * GPI + i, h, t], part)
                rows.append(part)
        return jnp.concatenate(rows, axis=0)

    def piece_copy(j, t, to_x):
        to = ((j % C) * 2 + t, zz * 2 + to_x)
        a = j // C
        return remote(
            parts.at[j, t, to_x], landed.at[a, me], p_send.at[j, t, to_x], p_recv.at[a, me], to
        )

    def piece_local(j):
        a = j // C
        return pltpu.make_async_copy(parts.at[j, k, x], landed.at[a, me], p_recv.at[a, me])

    def compute(j):
        keys, values = image_of(j, 0), image_of(j, 1)
        keys_t, values_t = keys.T, values.T
        wide = PAIR * BLK
        visible = lax.broadcasted_iota(jnp.int32, (SLOT, wide), 0) < count
        dk = jnp.zeros((SLOT, DH), jnp.float32)
        dv = jnp.zeros((SLOT, DH), jnp.float32)
        for first in range(0, GROUPS, PAIR):
            heads = [
                pl.ds(pl.multiple_of((j * GROUPS + h) * DH, DH), DH)
                for h in range(first, first + PAIR)
            ]
            q = jnp.concatenate([q_ref[:, h] for h in heads], axis=0)
            gr = jnp.concatenate(
                [(g_ref[:, h].astype(jnp.float32) * factor).astype(jnp.bfloat16) for h in heads],
                axis=0,
            )
            scores = jnp.where(visible, dot(keys, q, ROWS), -jnp.inf)
            top = jnp.max(scores, axis=0, keepdims=True)
            expo = jnp.exp2((scores - top) * (SCALE * LOG2E))
            weights = expo * (1.0 / jnp.sum(expo, axis=0, keepdims=True))
            low = weights.astype(jnp.bfloat16)
            dv += dot(low, gr)
            o_t = dot(values_t, low)
            wgrad = dot(values, gr, ROWS)
            centre = jnp.sum(weights * wgrad, axis=0, keepdims=True)
            sgrad = (weights * (wgrad - centre)).astype(jnp.bfloat16)
            dq_t = dot(keys_t, sgrad)
            dk += dot(sgrad, q)
            for i, h in enumerate(heads):
                cols = slice(i * BLK, (i + 1) * BLK)
                o_ref[:, h] = (o_t[:, cols].T * factor).astype(jnp.bfloat16)
                dq_ref[:, h] = (dq_t[:, cols].T * SCALE).astype(jnp.bfloat16)
        rr = SLOT // (GPI * S)
        for t, total in ((0, dk * SCALE), (1, dv)):
            total = total.reshape(GPI, Z, 2, rr, DH).astype(jnp.bfloat16)
            for to_x in range(2):
                parts[j, t, to_x] = total[:, :, to_x]

    def start_pieces(j):
        mine = j % C == c
        for t in range(2):
            for to_x in range(2):
                here = mine & (k == t) & (x == to_x)

                @pl.when(jnp.logical_not(here))
                def _():
                    piece_copy(j, t, to_x).start()

        @pl.when(mine)
        def _():
            piece_local(j).start()

    def wait_sent_pieces(j):
        mine = j % C == c
        for t in range(2):
            for to_x in range(2):
                here = mine & (k == t) & (x == to_x)

                @pl.when(jnp.logical_not(here))
                def _():
                    piece_copy(j, t, to_x).wait_send()

    def z_copy(a, d):
        to = (zz + d) % Z
        return remote(
            zsend.at[a, to], zrecv.at[a, d - 1], z_send.at[a, d - 1], z_recv.at[a, d - 1],
            (g, to * 2 + x),
        )

    def sum_images(j):
        a = j // C

        @pl.loop(0, 2 * G)
        def _(p):
            pltpu.make_async_copy(parts.at[0, 0, 0], landed.at[a, p], p_recv.at[a, p]).wait()

        @pl.loop(0, Z)
        def _(zt):
            sums = [None] * IMAGES
            for p in range(2 * G):
                piece = landed[a, p, :, zt].astype(jnp.float32)
                who = idbuf[p][0:1].reshape(1, 1, DH)
                for m in range(IMAGES):
                    term = jnp.where(who == m, piece, 0.0)
                    sums[m] = term if p == 0 else sums[m] + term
            for m in range(IMAGES):
                zsend[a, zt, m] = sums[m].astype(jnp.bfloat16)

        for d in range(1, Z):
            z_copy(a, d).start()

    def f_copy(a, d):
        to = (g + d) % G
        return remote(
            fsend.at[a, to], grads_ref.at[a, g], f_send.at[a, d - 1], f_recv.at[a, d - 1], (to, s)
        )

    def sum_z(j):
        a = j // C
        for d in range(1, Z):
            z_copy(a, d).wait_recv()
        total = zsend[a, zz].astype(jnp.float32)
        for d in range(1, Z):
            total += zrecv[a, d - 1].astype(jnp.float32)
        total = total.astype(jnp.bfloat16)
        for m in range(IMAGES):
            for i in range(GPI):
                fsend[a, m * GPI + i] = total[m, i]
        grads_ref[a, g] = fsend[a, g]
        for d in range(1, G):
            f_copy(a, d).start()

    @pl.loop(0, KVH + 2)
    def _(j):
        @pl.when(j < KVH)
        def _():
            @pl.when(j + 2 < KVH)
            def _():
                y_forward(j + 2)

            @pl.when(j + 1 < KVH)
            def _():
                x_forward(j + 1)

            sib_copy(j).wait_recv()
            for d in range(1, C):
                ys_copy(j, d).wait_recv()
                xs_copy(j, d).wait_recv()
            compute(j)
            start_pieces(j)

        @pl.when((j >= 1) & (j <= KVH) & ((j + C - 1) % C == c))
        def _():
            sum_images(j - 1)

        @pl.when((j >= 2) & ((j + 2 * C - 2) % C == c))
        def _():
            sum_z(j - 2)

    @pl.loop(0, KVH // C)
    def _(a):
        for d in range(1, G):
            f_copy(a, d).wait()
        for d in range(1, Z):
            z_copy(a, d).wait_send()

    @pl.loop(0, KVH)
    def _(j):
        sib_copy(j).wait_send()
        for d in range(1, C):
            y_copy(j, d).wait_send()
            ys_copy(j, d).wait_send()
            x_copy(j, d).wait_send()
            xs_copy(j, d).wait_send()
        wait_sent_pieces(j)


def per_device(queries, image_keys, image_values, gate_logit, block_image, image_counts, output_grad):
    G, S = lax.axis_size("grp"), lax.axis_size("seq")
    C, Z, GPI = G // 2, S // 2, G // IMAGES
    rows = queries.shape[0]
    assert rows == BLK and 2 * KVH % G == 0
    A = KVH // C
    rr = SLOT // (GPI * S)
    half = image_keys.shape[0] // 2
    smem = pl.BlockSpec(memory_space=pltpu.SMEM)
    vmem = pl.BlockSpec(memory_space=pltpu.VMEM)
    dma = pltpu.SemaphoreType.DMA
    bf16 = jnp.bfloat16
    attended, query_grad, grads = pl.pallas_call(
        functools.partial(kernel, G, S),
        in_specs=[smem] * 3 + [vmem] * 4,
        out_specs=[vmem] * 3,
        out_shape=[
            jax.ShapeDtypeStruct(queries.shape, bf16),
            jax.ShapeDtypeStruct(queries.shape, bf16),
            jax.ShapeDtypeStruct((A, G, rr, DH), bf16),
        ],
        scratch_shapes=[
            pltpu.VMEM((KVH, G, 2, 2, half, DH), bf16),
            pltpu.VMEM((2 * G, 8, DH), jnp.int32),
            pltpu.VMEM((KVH, 2, 2, GPI, Z, rr, DH), bf16),
            pltpu.VMEM((A, 2 * G, GPI, Z, rr, DH), bf16),
            pltpu.VMEM((A, Z, IMAGES, GPI, rr, DH), bf16),
            pltpu.VMEM((A, Z - 1, IMAGES, GPI, rr, DH), bf16),
            pltpu.VMEM((A, G, rr, DH), bf16),
            dma((2 * G - 1,)), dma((2 * G - 1,)),
            dma((KVH,)), dma((KVH,)),
        ]
        + [dma((KVH, C - 1))] * 8
        + [
            dma((KVH, 2, 2)), dma((A, 2 * G)),
            dma((A, Z - 1)), dma((A, Z - 1)),
            dma((A, G - 1)), dma((A, G - 1)),
        ],
        compiler_params=pltpu.CompilerParams(
            collective_id=0, has_side_effects=True, vmem_limit_bytes=48 << 20
        ),
        cost_estimate=pl.CostEstimate(
            flops=12 * rows * KVH * GROUPS * SLOT * DH,
            bytes_accessed=16 << 20,
            transcendentals=rows * KVH * GROUPS * SLOT,
        ),
    )(block_image, image_counts, gate_logit, queries, output_grad, image_keys, image_values)
    grads = grads.reshape(KVH, 2, rr, DH).transpose(1, 2, 0, 3).reshape(2, rr, KVH * DH)
    return attended, query_grad, grads[0], grads[1]


def solution(mesh):
    rows = P(("grp", "seq"), None)
    return jax.shard_map(
        per_device,
        mesh=mesh,
        in_specs=(rows, P("grp", None), P("grp", None), P(), P("grp", None), P(), rows),
        out_specs=(rows, rows, rows, rows),
        check_vma=False,
    )
```

time: 275 us -> 107 us (0.39)
  waiting for transfers between devices: 175 us -> 0 us
  Pallas kernels: 32.3 us -> 96.7 us
  blocking collectives: 32.8 us -> 0 us
  between operations: 15.2 us -> 1.31 us
  starting transfers between devices: 3.86 us -> 0 us
  local copies, waits for them, and re-layouts: 11.9 us -> 8.43 us
  other arithmetic: 3.35 us -> 0 us
    unnamed x4 -> x0, waiting for transfers between devices: 102 us -> none
    all_gather x2 -> x0, waiting for transfers between devices: 73 us -> none  [the longest x1 36.9 us: per_device(): keys = lax.all_gather(image_keys, 'grp', axis=0, tiled=True)]
    pallas_call x1, Pallas kernels: 32.3 us -> 96.7 us  [per_device(): pl.pallas_call(functools.partial(kernel, G, S), in_specs=[smem] * 3 + [vm...]
    unnamed x1 -> x0, blocking collectives: 24.3 us -> none
    all_to_all x1 -> x0, blocking collectives: 8.58 us -> none  [per_device(): whole = lax.all_to_all(mine, 'grp', split_axis=0, concat_axis=0, tiled=True)]
    all_to_all x1 -> x0, starting transfers between devices: 3.74 us -> none  [per_device(): lax.all_to_all(dkv.reshape(blocks, SLOT, grp, cols), 'grp', split_axis=2,...]
    reshape x4 -> x0, local copies, waits for them, and re-layouts: 3.36 us -> none  [the longest x1 1.62 us: per_device(): mine = mine.reshape(grp, out_rows, cols)]
    unnamed x18 -> x11, local copies, waits for them, and re-layouts: 5.69 us -> 7.5 us
  transfers between devices with their start and end apart: 4 -> 0, of which waited for: 3 -> 0; matrix products, arithmetic and copies ran while one was open for 1% -> 0% of each run, Pallas kernels for 0% -> 0%
where the time goes in v2:
time: 107 us; the launch traced here: 106 us
  Pallas kernels  96.7 us (90%)
  local copies, waits for them, and re-layouts  8.43 us (8%)
  between operations  1.31 us (1%)
    pallas_call x1, Pallas kernels, per_device(): pl.pallas_call(functools.partial(kernel, G, S), in_specs=[smem] * 3 + [vm...  96.7 us
    unnamed x11, local copies, waits for them, and re-layouts  7.5 us

profile of v2, /device:TPU:0, one launch (start us, length us, event | category | flops | bytes accessed | tf_op | source)
XLA Modules:
  0.0 106.4 jit_solution(3450650358637804405)
XLA Ops:
  1.3 0.7 copy.11.ids_ref
  2.0 0.0 copy-start
  2.0 1.2 %copy-done = bf16[512,1024]{1,0:T(8,128)(2,1)S(1)} copy-done((bf16[512,1024]{1,0:T(8,128)(2,1)S(1)}, bf16[512,1024]{1,0:T(8,128)(2,1)}, u32[]{:S(2)}) %copy-start) | copy-done | bytes 1048600
  3.2 0.0 copy-start.1
  3.2 1.2 %copy-done.1 = bf16[512,1024]{1,0:T(8,128)(2,1)S(1)} copy-done((bf16[512,1024]{1,0:T(8,128)(2,1)S(1)}, bf16[512,1024]{1,0:T(8,128)(2,1)}, u32[]{:S(2)}) %copy-start.1) | copy-done | bytes 1048600
  4.5 0.0 copy-start.2
  4.5 0.7 copy-done.2
  5.1 96.7 %shard_map.102 = (bf16[128,8192]{1,0:T(8,128)(2,1)S(1)}, bf16[128,8192]{1,0:T(8,128)(2,1)}, bf16[4,4,64,128]{3,2,1,0:T(8,128)(2,1)S(1)}) custom-call(s32[8,1]{1,0:T(8,128)S(1)} %copy.11.ids_ref, s32[4]{0:T(128)S(1)} %copy-done.2, f32[1]{0:T(128)S(6)} %copy.20.gate_ref, bf16[128,8192]{1,0:T(8,128)(2,1)} %q_ref.1, bf16[128,8192]{1,0:T(8,128)(2,1)} %g_ref.1, ...), custom_call_target="tpu_custom_call" | custom-call | flops 6442450944 | bytes 16777216 | tf_op jit(solution)/shard_map/pallas_call | solution.py:314
  101.8 0.1 copy.13
  101.9 0.1 copy.12
  102.0 0.7 copy_bitcast_fusion
  102.7 0.0 copy-start.3
  102.7 1.3 %copy.21 = bf16[128,8192]{1,0:T(8,128)(2,1)} copy(bf16[128,8192]{1,0:T(8,128)(2,1)S(1)} %get-tuple-element.18) | data formatting | bytes 4194304
  104.1 1.0 copy-done.3
  105.1 1.3 %copy.22 = bf16[128,8192]{1,0:T(8,128)(2,1)} copy(bf16[128,8192]{1,0:T(8,128)(2,1)S(1)} %copy-done.3) | data formatting | bytes 4194304
  (1 shorter events, 0.0 us)
Async XLA Ops:
  2.0 1.2 %copy-start = (bf16[512,1024]{1,0:T(8,128)(2,1)S(1)}, bf16[512,1024]{1,0:T(8,128)(2,1)}, u32[]{:S(2)}) copy-start(bf16[512,1024]{1,0:T(8,128)(2,1)} %k_ref.1) | copy-start | bytes 3145732
  3.2 1.2 %copy-start.1 = (bf16[512,1024]{1,0:T(8,128)(2,1)S(1)}, bf16[512,1024]{1,0:T(8,128)(2,1)}, u32[]{:S(2)}) copy-start(bf16[512,1024]{1,0:T(8,128)(2,1)} %v_ref.1) | copy-start | bytes 3145732
  4.5 0.7 copy-start.2
  102.7 2.3 %copy-start.3 = (bf16[128,8192]{1,0:T(8,128)(2,1)S(1)}, bf16[128,8192]{1,0:T(8,128)(2,1)}, u32[]{:S(2)}) copy-start(bf16[128,8192]{1,0:T(8,128)(2,1)} %get-tuple-element.19) | copy-start | bytes 6291460

commit v3 on v2

--- a/solution.py
+++ b/solution.py
@@ -34,9 +34,9 @@
 
 def kernel(
     G, S,
-    ids_ref, counts_ref, gate_ref, q_ref, g_ref, k_ref, v_ref,
+    ids_ref, counts_ref, gate_ref, q_hbm, g_hbm, k_ref, v_ref,
     o_ref, dq_ref, grads_ref,
-    kv, idbuf, parts, landed, zsend, zrecv, fsend,
+    q_ref, g_ref, in_sem, kv, idbuf, parts, landed, zsend, zrecv, fsend,
     id_send, id_recv, sib_send, sib_recv, y_send, y_recv, ys_send, ys_recv,
     x_send, x_recv, xs_send, xs_recv, p_send, p_recv, z_send, z_recv, f_send, f_recv,
 ):
@@ -50,11 +50,13 @@
     peers = [((g + d // 2) % G, zz * 2 + (x + d) % 2) for d in range(1, 2 * G)]
     zpeers = [(g, ((zz + d) % Z) * 2 + x) for d in range(1, Z)]
 
+    loads = [
+        pltpu.make_async_copy(src, dst, in_sem.at[i])
+        for i, (src, dst) in enumerate(((q_hbm, q_ref), (g_hbm, g_ref)))
+    ]
+    for load in loads:
+        load.start()
     half = k_ref.shape[0] // 2
-    for j in range(KVH):
-        for h in range(2):
-            kv[j, g, h, 0] = k_ref[h * half : (h + 1) * half, j * DH : (j + 1) * DH]
-            kv[j, g, h, 1] = v_ref[h * half : (h + 1) * half, j * DH : (j + 1) * DH]
     own = ids_ref[s, 0]
     me = g * 2 + x
     idbuf[me] = jnp.full((8, DH), own, jnp.int32)
@@ -89,14 +91,14 @@
     def id_copy(i):
         return remote(idbuf.at[me], idbuf.at[me], id_send.at[i], id_recv.at[i], peers[i])
 
-    @pl.loop(0, KVH)
-    def _(j):
+    def issue(j):
+        cols = pl.ds(pl.multiple_of(j * DH, DH), DH)
+        for h in range(2):
+            kv[j, g, h, 0] = k_ref[h * half : (h + 1) * half, cols]
+            kv[j, g, h, 1] = v_ref[h * half : (h + 1) * half, cols]
         for d in range(1, C):
             y_copy(j, d).start()
         sib_copy(j).start()
-
-    for i in range(len(peers)):
-        id_copy(i).start()
 
     def y_forward(j):
         for d in range(1, C):
@@ -109,11 +111,17 @@
             x_copy(j, d).wait_recv()
             xs_copy(j, d).start()
 
+    issue(0)
+    issue(1)
     y_forward(0)
+    issue(2)
     y_forward(1)
+    issue(3)
+    for i in range(len(peers)):
+        id_copy(i).start()
     x_forward(0)
-    for i in range(len(peers)):
-        id_copy(i).wait()
+    for load in loads:
+        load.wait()
 
     count = counts_ref[0]
     for m in range(1, IMAGES):
@@ -254,7 +262,7 @@
         for d in range(1, G):
             f_copy(a, d).start()
 
-    @pl.loop(0, KVH + 2)
+    @pl.loop(0, KVH + 4)
     def _(j):
         @pl.when(j < KVH)
         def _():
@@ -265,6 +273,10 @@
             @pl.when(j + 1 < KVH)
             def _():
                 x_forward(j + 1)
+
+            @pl.when(j + 4 < KVH)
+            def _():
+                issue(j + 4)
 
             sib_copy(j).wait_recv()
             for d in range(1, C):
@@ -273,13 +285,18 @@
             compute(j)
             start_pieces(j)
 
-        @pl.when((j >= 1) & (j <= KVH) & ((j + C - 1) % C == c))
-        def _():
-            sum_images(j - 1)
-
-        @pl.when((j >= 2) & ((j + 2 * C - 2) % C == c))
-        def _():
-            sum_z(j - 2)
+        @pl.when(j == 1)
+        def _():
+            for i in range(len(peers)):
+                id_copy(i).wait()
+
+        @pl.when((j >= 2) & (j < KVH + 2) & ((j + 2 * C - 2) % C == c))
+        def _():
+            sum_images(j - 2)
+
+        @pl.when((j >= 4) & ((j + 4 * C - 4) % C == c))
+        def _():
+            sum_z(j - 4)
 
     @pl.loop(0, KVH // C)
     def _(a):
@@ -309,11 +326,12 @@
     half = image_keys.shape[0] // 2
     smem = pl.BlockSpec(memory_space=pltpu.SMEM)
     vmem = pl.BlockSpec(memory_space=pltpu.VMEM)
+    hbm = pl.BlockSpec(memory_space=pltpu.HBM)
     dma = pltpu.SemaphoreType.DMA
     bf16 = jnp.bfloat16
     attended, query_grad, grads = pl.pallas_call(
         functools.partial(kernel, G, S),
-        in_specs=[smem] * 3 + [vmem] * 4,
+        in_specs=[smem] * 3 + [hbm] * 2 + [vmem] * 2,
         out_specs=[vmem] * 3,
         out_shape=[
             jax.ShapeDtypeStruct(queries.shape, bf16),
@@ -321,6 +339,9 @@
             jax.ShapeDtypeStruct((A, G, rr, DH), bf16),
         ],
         scratch_shapes=[
+            pltpu.VMEM(queries.shape, bf16),
+            pltpu.VMEM(queries.shape, bf16),
+            dma((2,)),
             pltpu.VMEM((KVH, G, 2, 2, half, DH), bf16),
             pltpu.VMEM((2 * G, 8, DH), jnp.int32),
             pltpu.VMEM((KVH, 2, 2, GPI, Z, rr, DH), bf16),

time: 107 us -> 88.8 us (0.83)
  Pallas kernels: 96.7 us -> 78.8 us
    pallas_call x1, Pallas kernels: 96.7 us -> 78.8 us  [per_device(): pl.pallas_call(functools.partial(kernel, G, S), in_specs=[smem] * 3 + [hb...]
where the time goes in v3:
time: 88.8 us; the launch traced here: 88.5 us
  Pallas kernels  78.8 us (89%)
  local copies, waits for them, and re-layouts  8.43 us (9%)
  between operations  1.31 us (1%)
    pallas_call x1, Pallas kernels, per_device(): pl.pallas_call(functools.partial(kernel, G, S), in_specs=[smem] * 3 + [hb...  78.8 us
    unnamed x11, local copies, waits for them, and re-layouts  7.5 us

profile of v3, /device:TPU:0, one launch (start us, length us, event | category | flops | bytes accessed | tf_op | source)
XLA Modules:
  0.0 88.5 jit_solution(8411542864536119883)
XLA Ops:
  1.3 0.7 copy.11.ids_ref
  2.0 0.0 copy-start
  2.0 1.2 %copy-done = bf16[512,1024]{1,0:T(8,128)(2,1)S(1)} copy-done((bf16[512,1024]{1,0:T(8,128)(2,1)S(1)}, bf16[512,1024]{1,0:T(8,128)(2,1)}, u32[]{:S(2)}) %copy-start) | copy-done | bytes 1048600
  3.2 0.0 copy-start.1
  3.2 1.2 %copy-done.1 = bf16[512,1024]{1,0:T(8,128)(2,1)S(1)} copy-done((bf16[512,1024]{1,0:T(8,128)(2,1)S(1)}, bf16[512,1024]{1,0:T(8,128)(2,1)}, u32[]{:S(2)}) %copy-start.1) | copy-done | bytes 1048600
  4.5 0.0 copy-start.2
  4.5 0.7 copy-done.2
  5.1 78.8 %shard_map.102 = (bf16[128,8192]{1,0:T(8,128)(2,1)S(1)}, bf16[128,8192]{1,0:T(8,128)(2,1)}, bf16[4,4,64,128]{3,2,1,0:T(8,128)(2,1)S(1)}) custom-call(s32[8,1]{1,0:T(8,128)S(1)} %copy.11.ids_ref, s32[4]{0:T(128)S(1)} %copy-done.2, f32[1]{0:T(128)S(6)} %copy.20.gate_ref, bf16[128,8192]{1,0:T(8,128)(2,1)} %q_hbm.1, bf16[128,8192]{1,0:T(8,128)(2,1)} %g_hbm.1, ...), custom_call_target="tpu_custom_call" | custom-call | flops 6442450944 | bytes 16777216 | tf_op jit(solution)/shard_map/pallas_call | solution.py:332
  83.9 0.1 copy.13
  84.0 0.1 copy.12
  84.1 0.7 copy_bitcast_fusion
  84.9 0.0 copy-start.3
  84.9 1.3 %copy.21 = bf16[128,8192]{1,0:T(8,128)(2,1)} copy(bf16[128,8192]{1,0:T(8,128)(2,1)S(1)} %get-tuple-element.18) | data formatting | bytes 4194304
  86.2 1.0 %copy-done.3 = bf16[128,8192]{1,0:T(8,128)(2,1)S(1)} copy-done((bf16[128,8192]{1,0:T(8,128)(2,1)S(1)}, bf16[128,8192]{1,0:T(8,128)(2,1)}, u32[]{:S(2)}) %copy-start.3) | copy-done | bytes 2097176
  87.2 1.3 %copy.22 = bf16[128,8192]{1,0:T(8,128)(2,1)} copy(bf16[128,8192]{1,0:T(8,128)(2,1)S(1)} %copy-done.3) | data formatting | bytes 4194304
  (1 shorter events, 0.0 us)
Async XLA Ops:
  2.0 1.2 %copy-start = (bf16[512,1024]{1,0:T(8,128)(2,1)S(1)}, bf16[512,1024]{1,0:T(8,128)(2,1)}, u32[]{:S(2)}) copy-start(bf16[512,1024]{1,0:T(8,128)(2,1)} %k_ref.1) | copy-start | bytes 3145732
  3.2 1.2 %copy-start.1 = (bf16[512,1024]{1,0:T(8,128)(2,1)S(1)}, bf16[512,1024]{1,0:T(8,128)(2,1)}, u32[]{:S(2)}) copy-start(bf16[512,1024]{1,0:T(8,128)(2,1)} %v_ref.1) | copy-start | bytes 3145732
  4.5 0.7 copy-start.2
  84.9 2.3 %copy-start.3 = (bf16[128,8192]{1,0:T(8,128)(2,1)S(1)}, bf16[128,8192]{1,0:T(8,128)(2,1)}, u32[]{:S(2)}) copy-start(bf16[128,8192]{1,0:T(8,128)(2,1)} %get-tuple-element.19) | copy-start | bytes 6291460

commit v4 on v3

--- a/solution.py
+++ b/solution.py
@@ -14,7 +14,7 @@
 IMAGES = 4
 BLK = 128
 GROUPS = 8
-PAIR = 2
+PAIR = 4
 SCALE = DH**-0.5
 LOG2E = math.log2(math.e)
 MESH = pl.DeviceIdType.MESH
@@ -34,11 +34,11 @@
 
 def kernel(
     G, S,
-    ids_ref, counts_ref, gate_ref, q_hbm, g_hbm, k_ref, v_ref,
+    ids_ref, counts_ref, gate_ref, q_hbm, g_hbm, k_hbm, v_hbm,
     o_ref, dq_ref, grads_ref,
-    q_ref, g_ref, in_sem, kv, idbuf, parts, landed, zsend, zrecv, fsend,
-    id_send, id_recv, sib_send, sib_recv, y_send, y_recv, ys_send, ys_recv,
-    x_send, x_recv, xs_send, xs_recv, p_send, p_recv, z_send, z_recv, f_send, f_recv,
+    q_ref, g_ref, k_ref, v_ref, in_sem, kv, idbuf, parts, landed, zsend, zrecv, fsend,
+    id_send, id_recv, sib_send, sib_recv, y_send, y_recv, x_send, x_recv, z1_send, z1_recv,
+    xz_send, xz_recv, zx_send, zx_recv, fwd_send, fwd_recv, p_send, p_recv, z_send, z_recv, f_send, f_recv,
 ):
     C, Z = G // 2, S // 2
     GPI = G // IMAGES
@@ -46,17 +46,21 @@
     c, k = g // 2, g % 2
     zz, x = s // 2, s % 2
     sib = (c * 2 + (1 - k), s)
+    zb = zz % 2
     xnb = (g, zz * 2 + (1 - x))
+    znb = (g, (zz + 1 - 2 * zb) * 2 + x)
     peers = [((g + d // 2) % G, zz * 2 + (x + d) % 2) for d in range(1, 2 * G)]
     zpeers = [(g, ((zz + d) % Z) * 2 + x) for d in range(1, Z)]
 
     loads = [
         pltpu.make_async_copy(src, dst, in_sem.at[i])
-        for i, (src, dst) in enumerate(((q_hbm, q_ref), (g_hbm, g_ref)))
+        for i, (src, dst) in enumerate(
+            ((k_hbm, k_ref), (v_hbm, v_ref), (q_hbm, q_ref), (g_hbm, g_ref))
+        )
     ]
     for load in loads:
         load.start()
-    half = k_ref.shape[0] // 2
+    eighth = k_ref.shape[0] // 8
     own = ids_ref[s, 0]
     me = g * 2 + x
     idbuf[me] = jnp.full((8, DH), own, jnp.int32)
@@ -69,33 +73,43 @@
     def sib_copy(j):
         return remote(kv.at[j, g], kv.at[j, g], sib_send.at[j], sib_recv.at[j], sib)
 
+    def source(d):
+        return ((c + C - d) % C) * 2 + k
+
+    def copy(ref, sems, j, d, to):
+        return remote(ref, ref, sems[0].at[j, d - 1], sems[1].at[j, d - 1], to)
+
     def y_copy(j, d):
         to = (((c + d) % C) * 2 + k, s)
-        return remote(kv.at[j, g, x], kv.at[j, g, x], y_send.at[j, d - 1], y_recv.at[j, d - 1], to)
-
-    def source(d):
-        return ((c + C - d) % C) * 2 + k
-
-    def ys_copy(j, d):
-        ref = kv.at[j, source(d), x]
-        return remote(ref, ref, ys_send.at[j, d - 1], ys_recv.at[j, d - 1], sib)
+        return copy(kv.at[j, g, x, zb], (y_send, y_recv), j, d, to)
 
     def x_copy(j, d):
-        ref = kv.at[j, source(d), x]
-        return remote(ref, ref, x_send.at[j, d - 1], x_recv.at[j, d - 1], xnb)
-
-    def xs_copy(j, d):
-        ref = kv.at[j, source(d), 1 - x]
-        return remote(ref, ref, xs_send.at[j, d - 1], xs_recv.at[j, d - 1], sib)
+        return copy(kv.at[j, source(d), x, zb], (x_send, x_recv), j, d, xnb)
+
+    def z1_copy(j, d):
+        return copy(kv.at[j, source(d), x, zb], (z1_send, z1_recv), j, d, znb)
+
+    def xz_copy(j, d):
+        return copy(kv.at[j, source(d), 1 - x, zb, 0], (xz_send, xz_recv), j, d, znb)
+
+    def zx_copy(j, d):
+        return copy(kv.at[j, source(d), x, 1 - zb, 1], (zx_send, zx_recv), j, d, xnb)
+
+    def fwd_copy(j, d, xh, zh):
+        return copy(kv.at[j, source(d), xh, zh], (fwd_send, fwd_recv), j, d, sib)
+
+    def fwd_all(j, d):
+        return copy(kv.at[j, source(d)], (fwd_send, fwd_recv), j, d, sib)
 
     def id_copy(i):
         return remote(idbuf.at[me], idbuf.at[me], id_send.at[i], id_recv.at[i], peers[i])
 
     def issue(j):
         cols = pl.ds(pl.multiple_of(j * DH, DH), DH)
-        for h in range(2):
-            kv[j, g, h, 0] = k_ref[h * half : (h + 1) * half, cols]
-            kv[j, g, h, 1] = v_ref[h * half : (h + 1) * half, cols]
+        for i in range(8):
+            part = slice(i * eighth, (i + 1) * eighth)
+            kv[j, g, i // 4, i // 2 % 2, i % 2, 0] = k_ref[part, cols]
+            kv[j, g, i // 4, i // 2 % 2, i % 2, 1] = v_ref[part, cols]
         for d in range(1, C):
             y_copy(j, d).start()
         sib_copy(j).start()
@@ -104,23 +118,40 @@
         for d in range(1, C):
             y_copy(j, d).wait_recv()
             x_copy(j, d).start()
-            ys_copy(j, d).start()
-
-    def x_forward(j):
+            z1_copy(j, d).start()
+            fwd_copy(j, d, x, zb).start()
+
+    def xz_forward(j):
         for d in range(1, C):
             x_copy(j, d).wait_recv()
-            xs_copy(j, d).start()
-
+            xz_copy(j, d).start()
+            fwd_copy(j, d, 1 - x, zb).start()
+            z1_copy(j, d).wait_recv()
+            zx_copy(j, d).start()
+            fwd_copy(j, d, x, 1 - zb).start()
+
+    def last_forward(j):
+        for d in range(1, C):
+            xz_copy(j, d).wait_recv()
+            zx_copy(j, d).wait_recv()
+            fwd_copy(j, d, 1 - x, 1 - zb).start()
+
+    for load in loads[:2]:
+        load.wait()
     issue(0)
     issue(1)
     y_forward(0)
     issue(2)
     y_forward(1)
+    xz_forward(0)
     issue(3)
+    y_forward(2)
+    issue(4)
     for i in range(len(peers)):
         id_copy(i).start()
-    x_forward(0)
-    for load in loads:
+    xz_forward(1)
+    last_forward(0)
+    for load in loads[2:]:
         load.wait()
 
     count = counts_ref[0]
@@ -131,15 +162,22 @@
     def image_of(j, t):
         rows = []
         for i in range(GPI):
-            for h in range(2):
-                part = kv[j, i, h, t]
+            for n in range(8):
+                at = (n // 4, n // 2 % 2, n % 2, t)
+                part = kv[(j, i) + at]
                 for m in range(1, IMAGES):
-                    part = jnp.where(own == m, kv[j, m * GPI + i, h, t], part)
+                    part = jnp.where(own == m, kv[(j, m * GPI + i) + at], part)
                 rows.append(part)
         return jnp.concatenate(rows, axis=0)
 
+    half = C // 2
+    kind = c // half
+
+    def owner(j, t):
+        return (t * half + j // 2 % half) * 2 + j % 2
+
     def piece_copy(j, t, to_x):
-        to = ((j % C) * 2 + t, zz * 2 + to_x)
+        to = (owner(j, t), zz * 2 + to_x)
         a = j // C
         return remote(
             parts.at[j, t, to_x], landed.at[a, me], p_send.at[j, t, to_x], p_recv.at[a, me], to
@@ -147,7 +185,7 @@
 
     def piece_local(j):
         a = j // C
-        return pltpu.make_async_copy(parts.at[j, k, x], landed.at[a, me], p_recv.at[a, me])
+        return pltpu.make_async_copy(parts.at[j, kind, x], landed.at[a, me], p_recv.at[a, me])
 
     def compute(j):
         keys, values = image_of(j, 0), image_of(j, 1)
@@ -189,10 +227,10 @@
                 parts[j, t, to_x] = total[:, :, to_x]
 
     def start_pieces(j):
-        mine = j % C == c
+        mine = owner(j, kind) == g
         for t in range(2):
             for to_x in range(2):
-                here = mine & (k == t) & (x == to_x)
+                here = (owner(j, t) == g) & (x == to_x)
 
                 @pl.when(jnp.logical_not(here))
                 def _():
@@ -203,10 +241,10 @@
             piece_local(j).start()
 
     def wait_sent_pieces(j):
-        mine = j % C == c
+        mine = owner(j, kind) == g
         for t in range(2):
             for to_x in range(2):
-                here = mine & (k == t) & (x == to_x)
+                here = (owner(j, t) == g) & (x == to_x)
 
                 @pl.when(jnp.logical_not(here))
                 def _():
@@ -238,8 +276,9 @@
             for m in range(IMAGES):
                 zsend[a, zt, m] = sums[m].astype(jnp.bfloat16)
 
-        for d in range(1, Z):
-            z_copy(a, d).start()
+            @pl.when(zt != zz)
+            def _():
+                z_copy(a, (zt + Z - zz) % Z).start()
 
     def f_copy(a, d):
         to = (g + d) % G
@@ -266,22 +305,25 @@
     def _(j):
         @pl.when(j < KVH)
         def _():
+            @pl.when(j + 3 < KVH)
+            def _():
+                y_forward(j + 3)
+
             @pl.when(j + 2 < KVH)
             def _():
-                y_forward(j + 2)
+                xz_forward(j + 2)
 
             @pl.when(j + 1 < KVH)
             def _():
-                x_forward(j + 1)
-
-            @pl.when(j + 4 < KVH)
+                last_forward(j + 1)
+
+            @pl.when(j + 5 < KVH)
             def _():
-                issue(j + 4)
+                issue(j + 5)
 
             sib_copy(j).wait_recv()
             for d in range(1, C):
-                ys_copy(j, d).wait_recv()
-                xs_copy(j, d).wait_recv()
+                fwd_all(j, d).wait_recv()
             compute(j)
             start_pieces(j)
 
@@ -290,11 +332,11 @@
             for i in range(len(peers)):
                 id_copy(i).wait()
 
-        @pl.when((j >= 2) & (j < KVH + 2) & ((j + 2 * C - 2) % C == c))
+        @pl.when((j >= 2) & (j < KVH + 2) & (owner((j + KVH - 2) % KVH, kind) == g))
         def _():
             sum_images(j - 2)
 
-        @pl.when((j >= 4) & ((j + 4 * C - 4) % C == c))
+        @pl.when((j >= 4) & (owner((j + KVH - 4) % KVH, kind) == g))
         def _():
             sum_z(j - 4)
 
@@ -309,10 +351,8 @@
     def _(j):
         sib_copy(j).wait_send()
         for d in range(1, C):
-            y_copy(j, d).wait_send()
-            ys_copy(j, d).wait_send()
-            x_copy(j, d).wait_send()
-            xs_copy(j, d).wait_send()
+            for each in (y_copy, x_copy, z1_copy, xz_copy, zx_copy, fwd_all):
+                each(j, d).wait_send()
         wait_sent_pieces(j)
 
 
@@ -323,7 +363,7 @@
     assert rows == BLK and 2 * KVH % G == 0
     A = KVH // C
     rr = SLOT // (GPI * S)
-    half = image_keys.shape[0] // 2
+    eighth = image_keys.shape[0] // 8
     smem = pl.BlockSpec(memory_space=pltpu.SMEM)
     vmem = pl.BlockSpec(memory_space=pltpu.VMEM)
     hbm = pl.BlockSpec(memory_space=pltpu.HBM)
@@ -331,7 +371,7 @@
     bf16 = jnp.bfloat16
     attended, query_grad, grads = pl.pallas_call(
         functools.partial(kernel, G, S),
-        in_specs=[smem] * 3 + [hbm] * 2 + [vmem] * 2,
+        in_specs=[smem] * 3 + [hbm] * 4,
         out_specs=[vmem] * 3,
         out_shape=[
             jax.ShapeDtypeStruct(queries.shape, bf16),
@@ -341,8 +381,10 @@
         scratch_shapes=[
             pltpu.VMEM(queries.shape, bf16),
             pltpu.VMEM(queries.shape, bf16),
-            dma((2,)),
-            pltpu.VMEM((KVH, G, 2, 2, half, DH), bf16),
+            pltpu.VMEM(image_keys.shape, bf16),
+            pltpu.VMEM(image_keys.shape, bf16),
+            dma((4,)),
+            pltpu.VMEM((KVH, G, 2, 2, 2, 2, eighth, DH), bf16),
             pltpu.VMEM((2 * G, 8, DH), jnp.int32),
             pltpu.VMEM((KVH, 2, 2, GPI, Z, rr, DH), bf16),
             pltpu.VMEM((A, 2 * G, GPI, Z, rr, DH), bf16),
@@ -352,7 +394,7 @@
             dma((2 * G - 1,)), dma((2 * G - 1,)),
             dma((KVH,)), dma((KVH,)),
         ]
-        + [dma((KVH, C - 1))] * 8
+        + [dma((KVH, C - 1))] * 12
         + [
             dma((KVH, 2, 2)), dma((A, 2 * G)),
             dma((A, Z - 1)), dma((A, Z - 1)),
@@ -367,7 +409,8 @@
             transcendentals=rows * KVH * GROUPS * SLOT,
         ),
     )(block_image, image_counts, gate_logit, queries, output_grad, image_keys, image_values)
-    grads = grads.reshape(KVH, 2, rr, DH).transpose(1, 2, 0, 3).reshape(2, rr, KVH * DH)
+    grads = grads.reshape(A, 2, C // 2, 2, rr, DH).transpose(1, 4, 0, 2, 3, 5)
+    grads = grads.reshape(2, rr, KVH * DH)
     return attended, query_grad, grads[0], grads[1]
 
 

time: 88.8 us -> 82.2 us (0.926)
  Pallas kernels: 78.8 us -> 71.4 us
    pallas_call x1, Pallas kernels: 78.8 us -> 71.4 us  [per_device(): pl.pallas_call(functools.partial(kernel, G, S), in_specs=[smem] * 3 + [hb...]
where the time goes in v4:
time: 82.2 us; the launch traced here: 81.9 us
  Pallas kernels  71.4 us (87%)
  local copies, waits for them, and re-layouts  9.25 us (11%)
  between operations  1.31 us (2%)
    pallas_call x1, Pallas kernels, per_device(): pl.pallas_call(functools.partial(kernel, G, S), in_specs=[smem] * 3 + [hb...  71.4 us
    unnamed x11, local copies, waits for them, and re-layouts  7.5 us

profile of v4, /device:TPU:0, one launch (start us, length us, event | category | flops | bytes accessed | tf_op | source)
XLA Modules:
  0.0 81.9 jit_solution(17581160235235210074)
XLA Ops:
  1.3 0.7 copy.11.ids_ref
  2.0 0.0 copy-start
  2.0 1.2 %copy-done = bf16[512,1024]{1,0:T(8,128)(2,1)S(1)} copy-done((bf16[512,1024]{1,0:T(8,128)(2,1)S(1)}, bf16[512,1024]{1,0:T(8,128)(2,1)}, u32[]{:S(2)}) %copy-start) | copy-done | bytes 1048600
  3.2 0.0 copy-start.1
  3.2 1.2 %copy-done.1 = bf16[512,1024]{1,0:T(8,128)(2,1)S(1)} copy-done((bf16[512,1024]{1,0:T(8,128)(2,1)S(1)}, bf16[512,1024]{1,0:T(8,128)(2,1)}, u32[]{:S(2)}) %copy-start.1) | copy-done | bytes 1048600
  4.5 0.0 copy-start.2
  4.5 0.7 copy-done.2
  5.1 71.4 %shard_map.102 = (bf16[128,8192]{1,0:T(8,128)(2,1)S(1)}, bf16[128,8192]{1,0:T(8,128)(2,1)}, bf16[4,4,64,128]{3,2,1,0:T(8,128)(2,1)S(1)}) custom-call(s32[8,1]{1,0:T(8,128)S(1)} %copy.11.ids_ref, s32[4]{0:T(128)S(1)} %copy-done.2, f32[1]{0:T(128)S(6)} %copy.16.gate_ref, bf16[128,8192]{1,0:T(8,128)(2,1)} %q_hbm.1, bf16[128,8192]{1,0:T(8,128)(2,1)} %g_hbm.1, ...), custom_call_target="tpu_custom_call" | custom-call | flops 6442450944 | bytes 16777216 | tf_op jit(solution)/shard_map/pallas_call | solution.py:372
  76.5 0.1 copy.13
  76.7 0.7 squeeze.7
  77.4 0.1 copy.12
  77.6 0.7 squeeze.6
  78.3 0.0 copy-start.3
  78.3 1.3 %copy.17 = bf16[128,8192]{1,0:T(8,128)(2,1)} copy(bf16[128,8192]{1,0:T(8,128)(2,1)S(1)} %get-tuple-element.16) | data formatting | bytes 4194304
  79.6 1.0 %copy-done.3 = bf16[128,8192]{1,0:T(8,128)(2,1)S(1)} copy-done((bf16[128,8192]{1,0:T(8,128)(2,1)S(1)}, bf16[128,8192]{1,0:T(8,128)(2,1)}, u32[]{:S(2)}) %copy-start.3) | copy-done | bytes 2097176
  80.6 1.3 %copy.18 = bf16[128,8192]{1,0:T(8,128)(2,1)} copy(bf16[128,8192]{1,0:T(8,128)(2,1)S(1)} %copy-done.3) | data formatting | bytes 4194304
  (1 shorter events, 0.0 us)
Async XLA Ops:
  2.0 1.2 %copy-start = (bf16[512,1024]{1,0:T(8,128)(2,1)S(1)}, bf16[512,1024]{1,0:T(8,128)(2,1)}, u32[]{:S(2)}) copy-start(bf16[512,1024]{1,0:T(8,128)(2,1)} %k_hbm.1) | copy-start | bytes 3145732
  3.2 1.2 %copy-start.1 = (bf16[512,1024]{1,0:T(8,128)(2,1)S(1)}, bf16[512,1024]{1,0:T(8,128)(2,1)}, u32[]{:S(2)}) copy-start(bf16[512,1024]{1,0:T(8,128)(2,1)} %v_hbm.1) | copy-start | bytes 3145732
  4.5 0.7 copy-start.2
  78.3 2.3 %copy-start.3 = (bf16[128,8192]{1,0:T(8,128)(2,1)S(1)}, bf16[128,8192]{1,0:T(8,128)(2,1)}, u32[]{:S(2)}) copy-start(bf16[128,8192]{1,0:T(8,128)(2,1)} %get-tuple-element.17) | copy-start | bytes 6291460
